TPU v7x, 32 devices: a whole 2x2x4 slice. The times are simulated.
32 devices in a mesh: grp: 1, row: 32 (over z, y, x, core), ka: 1.
Axes of the slice: x: 2, y: 2, z: 4, core: 2. Of those that a mesh axis runs over, the one named last changes fastest.
Arguments:
- pair_rep: bfloat16 [128, 128, 128], P(('grp', 'row'), 'ka'), may hold values from -6 to 6
- pair_mask: int32 [128, 128], P(('grp', 'row'), 'ka'), may hold values from 0 to 1, as said below
- proj_weight: bfloat16 [2, 128, 512], replicated, may hold values from -0.5 to 0.5
- proj_bias: float32 [2, 512], replicated, may hold values from -4 to 4
- gate_weight: bfloat16 [2, 128, 128], replicated, may hold values from -0.5 to 0.5
- gate_bias: float32 [2, 128], replicated, may hold values from -4 to 4
- out_weight: bfloat16 [2, 128, 128], replicated, may hold values from -0.5 to 0.5
- out_bias: float32 [2, 128], replicated, may hold values from -3 to 3
- norm_scale: float32 [2, 2, 128], replicated, may hold values from 0.1 to 1.9
- norm_offset: float32 [2, 2, 128], replicated, may hold values from -3 to 3
Outputs:
- pair_out: bfloat16 [128, 128, 128], P(('grp', 'row'), 'ka')
Inputs may be any that keep to these rules, and one draw needn't show every extreme that they name: pair_mask[a, b] is 1 wherever the circular residue distance min(|a - b|, 128 - |a - b|) is under 2 * 4; elsewhere it is 0 or 1.
All inputs are finite; a program needn't handle non-finite values.
Results may differ from a plain program's by a relative error of at most 0.014.
Values may be sent and summed in bfloat16 or wider, within the bound.
No kernel may reach another device: no remote copies, remote signals or barrier semaphores. Data moves between devices by JAX's collectives and lax.ppermute only.
A program may use at most 128 MiB of HBM per device.

v0:
```python
import functools

import jax
import jax.numpy as jnp
from jax import lax
from jax.experimental import pallas as pl
from jax.experimental.pallas import tpu as pltpu
from jax.sharding import PartitionSpec as P

PEERS = ("row", "ka")
OWN = 4
EACH = 16
BF16, F32 = jnp.bfloat16, jnp.float32


def over_rows(a, b):
    return lax.dot_general(a, b, (((0,), (0,)), ((), ())), preferred_element_type=F32)


def over_columns(a, b):
    return lax.dot_general(a, b, (((1,), (1,)), ((), ())), preferred_element_type=F32)


def layer_norm(values, norm_gain, norm_bias):
    average = jnp.mean(values, 0, keepdims=True)
    centred = values - average
    variance = jnp.mean(centred * centred, 0, keepdims=True)
    return centred * lax.rsqrt(variance + 1e-05) * norm_gain + norm_bias


def pack(blocks):
    channels, width = blocks[0].shape
    tiles = [b.reshape(channels // 8, 8, width) for b in blocks]
    turned = [pltpu.roll(b, 4, axis=0).reshape(channels // 8, 8, width) for b in blocks]
    low = lax.broadcasted_iota(jnp.int32, tiles[0].shape, 1) < 4
    back = [pltpu.roll(b, channels - 4, axis=0).reshape(channels // 8, 8, width) for b in blocks]
    even = [jnp.where(low, tiles[n], turned[n + 1]) for n in (0, 2)]
    odd = [jnp.where(low, back[n], tiles[n + 1]) for n in (0, 2)]
    return jnp.stack([jnp.stack(even, 1), jnp.stack(odd, 1)], 1).reshape(channels // 4, 16, width)


def unpack(packed):
    count, _, width = packed.shape
    tiles = packed.reshape(count // 2, 2, 2, 8, width)
    low = lax.broadcasted_iota(jnp.int32, (count // 2, 8, width), 1) < 4
    blocks = []
    for n in range(2):
        even, odd = tiles[:, 0, n], tiles[:, 1, n]
        down = pltpu.roll(odd.reshape(count * 4, width), 4, axis=0).reshape(even.shape)
        up = pltpu.roll(even.reshape(count * 4, width), count * 4 - 4, axis=0).reshape(even.shape)
        blocks.append(jnp.where(low, even, down).reshape(count * 4, width))
        blocks.append(jnp.where(low, up, odd).reshape(count * 4, width))
    return blocks


def sigmoid(x):
    return 0.5 * jnp.tanh(0.5 * x) + 0.5


def broadcast_columns(columns, first, many, width):
    held = columns[...]
    return [jnp.broadcast_to(held[:, n : n + 1], (held.shape[0], width)) for n in range(first, first + many)]


def project(u, z, mask, proj_weight, gate_weight, columns, send, gate, mixed):
    width = z[0].shape[1]
    h = proj_weight.shape[1] // 4
    rows = mixed.shape[1]
    gain, offset, *biases = broadcast_columns(columns, u * EACH, 7, width)
    turned = [proj_weight[:, n * h : (n + 1) * h].T for n in range(4)] + [gate_weight.T]
    for pair in range(0, OWN, 2):
        normed = [layer_norm(z[i], gain, offset).astype(BF16) for i in (pair, pair + 1)]
        normed = jnp.concatenate(normed, 1)
        both = [jnp.dot(w, normed, preferred_element_type=F32) for w in turned]
        for n in range(2):
            i = pair + n
            parts = [v[:, n * width : (n + 1) * width] + b for v, b in zip(both, biases)]
            keep = mask[i : i + 1, :]
            mixed[0, pl.ds(i, h, stride=OWN), :] = keep * sigmoid(parts[1]) * parts[0]
            mixed[1, pl.ds(i, h, stride=OWN), :] = keep * sigmoid(parts[3]) * parts[2]
            gate[:, i * width : (i + 1) * width] = sigmoid(parts[4])
    send[:, 0:16, :] = mixed[0].reshape(rows // 16, 16, width).astype(BF16)
    send[:, 16:32, :] = mixed[1].reshape(rows // 16, 16, width).astype(BF16)


def finish(u, z, summed, gate, out_weight, columns, mixed):
    width = z[0].shape[1]
    gain, offset, bias = broadcast_columns(columns, u * EACH + 7, 3, width)
    turned = out_weight.T
    mixed[...] = summed[...].astype(F32).reshape(mixed.shape)
    results = []
    for pair in range(0, OWN, 2):
        blocks = [mixed[pl.ds(i, mixed.shape[0] // OWN, stride=OWN), :] for i in (pair, pair + 1)]
        hidden = jnp.concatenate([layer_norm(v, gain, offset).astype(BF16) for v in blocks], 1)
        both = jnp.dot(turned, hidden, preferred_element_type=F32)
        for n in range(2):
            change = both[:, n * width : (n + 1) * width] + bias
            at = slice((pair + n) * width, (pair + n + 1) * width)
            results.append((z[pair + n].astype(F32) + gate[:, at] * change).astype(BF16))
    return results


def first_kernel(
    pair, mask, pw, gw, pb, gb, ob, ns, no, send, gate, turned, columns, keep, pair_in, mask_in, pw_in, gw_in, pb_in, gb_in, ob_in, ns_in, no_in, rows, arrived, mixed
):
    moves = [(pair, pair_in), (pb, pb_in), (gb, gb_in), (ob, ob_in), (ns, ns_in), (no, no_in)]
    moves += [(pw.at[0], pw_in), (gw.at[0], gw_in), (mask, mask_in)]
    moves = [pltpu.make_async_copy(a, b, arrived.at[n]) for n, (a, b) in enumerate(moves)]
    for move in moves:
        move.start()
    moves[0].wait()
    width = pair.shape[1]
    z = [pair_in[i].T for i in range(OWN)]
    for i in range(OWN):
        turned[:, i * width : (i + 1) * width] = z[i]
    for move in moves[1:6]:
        move.wait()
    h = pw.shape[2] // 4
    for u in range(2):
        found = [ns_in[u, 0:1, :], no_in[u, 0:1, :]] + [pb_in[u : u + 1, n * h : (n + 1) * h] for n in range(4)]
        found += [gb_in[u : u + 1, :], ns_in[u, 1:2, :], no_in[u, 1:2, :], ob_in[u : u + 1, :]]
        for n, row in enumerate(found):
            rows[u * EACH + n : u * EACH + n + 1, :] = row
    columns[...] = rows[...].T
    for move in moves[6:]:
        move.wait()
    keep[0:OWN, :] = mask_in[...].astype(F32)
    project(0, [v.astype(F32) for v in z], keep, pw_in[...], gw_in[...], columns, send, gate, mixed)


def middle_kernel(summed, old, old_gate, columns, keep, pw, gw, ow, send, gate, turned, mixed, mixed_back):
    width = keep.shape[1]
    z = finish(0, [old[:, i * width : (i + 1) * width] for i in range(OWN)], summed, old_gate, ow[0], columns, mixed_back)
    for i in range(OWN):
        turned[:, i * width : (i + 1) * width] = z[i]
    project(1, [v.astype(F32) for v in z], keep, pw[1], gw[1], columns, send, gate, mixed)


def last_kernel(summed, old, old_gate, columns, ow, out, mixed_back):
    width = out.shape[1]
    z = finish(1, [old[:, i * width : (i + 1) * width] for i in range(OWN)], summed, old_gate, ow[1], columns, mixed_back)
    for i in range(OWN):
        out[i] = z[i].T


def triangle_kernel(incoming, sides, out):
    left, right = [unpack(sides[:, n : n + 16, :].astype(F32)) for n in (0, 16)]
    product = over_rows if incoming else over_columns
    out[...] = pack([product(a.astype(BF16), b.astype(BF16)) for a, b in zip(left, right)]).astype(BF16)


def call(kernel, outs, scratch, *args, place=pltpu.VMEM):
    in_vmem = pl.BlockSpec(memory_space=pltpu.VMEM)
    return pl.pallas_call(
        kernel,
        out_shape=[jax.ShapeDtypeStruct(*o) for o in outs],
        in_specs=[pl.BlockSpec(memory_space=place)] * len(args),
        out_specs=[in_vmem] * len(outs),
        scratch_shapes=scratch,
        compiler_params=pltpu.CompilerParams(vmem_limit_bytes=24 * 2**20),
    )(*args)


def exchange(blocks):
    return lax.all_to_all(blocks, PEERS, split_axis=0, concat_axis=0, tiled=True)


def packed_updates(count, pair_rep, pair_mask, pw, pb, gw, gb, ow, ob, ns, no):
    rows_of, width, channels = pair_rep.shape
    flat = (channels, rows_of * width)
    projected = [((count, 32, width), BF16), (flat, F32), (flat, BF16)]
    summed = [((count, 16, width), BF16)]
    params = [pair_rep, pair_mask, pw, gw, pb, gb, ob, ns, no]
    params = [pltpu.with_memory_space_constraint(v, pltpu.HBM) for v in params]
    held = [pltpu.VMEM(v.shape[1:] if n in (2, 3) else v.shape, v.dtype) for n, v in enumerate(params)]
    held += [pltpu.VMEM((2 * EACH, channels), F32), pltpu.SemaphoreType.DMA((len(params),))]
    back = pltpu.VMEM((OWN * channels, width), F32)
    mixed = pltpu.VMEM((2, OWN * channels, width), F32)
    kept = [((channels, 2 * EACH), F32), ((2 * OWN, width), F32)]
    send, gate, turned, columns, keep = call(first_kernel, projected + kept, held + [mixed], *params, place=pltpu.HBM)
    (send,) = call(functools.partial(triangle_kernel, False), summed, [], exchange(send))
    send, gate, turned = call(middle_kernel, projected, [mixed, back], exchange(send), turned, gate, columns, keep, pw, gw, ow)
    (send,) = call(functools.partial(triangle_kernel, True), summed, [], exchange(send))
    (out,) = call(last_kernel, [(pair_rep.shape, BF16)], [back], exchange(send), turned, gate, columns, ow)
    return out


def update(pair_t, pair_mask, u, incoming, peers, rows_of, pw, pb, gw, gb, ow, ob, ns, no):
    channels, positions = pair_t.shape
    width = positions // rows_of
    h = pw.shape[2] // 4
    count = peers[0] * peers[1]
    own = h // count
    normed = layer_norm(pair_t, ns[u, 0][:, None], no[u, 0][:, None]).astype(BF16)
    projected = over_rows(jnp.concatenate([pw[u], gw[u]], 1), normed) + jnp.concatenate([pb[u], gb[u]], 0)[:, None]
    parts = [projected[n * h : (n + 1) * h] for n in range(4)]
    gating = jax.nn.sigmoid(projected[4 * h :])
    mask = pair_mask.astype(F32).reshape(1, positions)
    left = (mask * jax.nn.sigmoid(parts[1]) * parts[0]).astype(BF16)
    right = (mask * jax.nn.sigmoid(parts[3]) * parts[2]).astype(BF16)
    sides = exchange(jnp.stack([v.reshape(count, own, rows_of, width) for v in (left, right)], 1))
    sides = sides.reshape(peers[0], peers[1], 2, own, rows_of, width)
    sides = sides.transpose(2, 3, 0, 4, 1, 5).reshape(2, own, peers[0] * rows_of, peers[1] * width)
    form = "cki,ckj->cij" if incoming else "cik,cjk->cij"
    summed = jnp.einsum(form, sides[0], sides[1], preferred_element_type=F32).astype(BF16)
    summed = summed.reshape(own, peers[0], rows_of, peers[1], width).transpose(1, 3, 0, 2, 4)
    summed = exchange(summed.reshape(count, own, rows_of, width)).reshape(h, positions).astype(F32)
    hidden = layer_norm(summed, ns[u, 1][:, None], no[u, 1][:, None]).astype(BF16)
    change = over_rows(ow[u], hidden) + ob[u][:, None]
    return (pair_t + gating * change).astype(BF16)


def plain_updates(peers, pair_rep, pair_mask, *params):
    rows_of, width, channels = pair_rep.shape
    pair_t = pair_rep.reshape(rows_of * width, channels).T
    for u in range(2):
        pair_t = update(pair_t.astype(F32), pair_mask, u, u == 1, peers, rows_of, *params)
    return pair_t.T.reshape(rows_of, width, channels)


def solution(mesh):
    peers = (mesh.shape["row"], mesh.shape["ka"])
    count = peers[0] * peers[1]

    def on_device(pair_rep, pair_mask, *params):
        rows_of, width, channels = pair_rep.shape
        hidden = params[0].shape[2] // 4
        fits = peers[1] == 1 and rows_of == OWN and hidden == OWN * count and count % 2 == 0
        if fits and channels == hidden == 128 and width % 128 == 0:
            return packed_updates(count, pair_rep, pair_mask, *params)
        return plain_updates(peers, pair_rep, pair_mask, *params)

    split = P(("grp", "row"), "ka", None)
    in_specs = (split, P(("grp", "row"), "ka")) + (P(),) * 8
    return jax.shard_map(on_device, mesh=mesh, in_specs=in_specs, out_specs=split, check_vma=False)
```

profile of v0, /device:TPU:0, one launch (start us, length us, event | category | flops | bytes accessed | tf_op | source)
XLA Modules:
  0.0 55.0 jit_solution(12313570226766494869)
XLA Ops:
  0.0 1.7 %shard_map.100 = (bf16[32,32,128]{2,1,0:T(8,128)(2,1)S(1)}, f32[128,512]{1,0:T(8,128)S(1)}, bf16[128,512]{1,0:T(8,128)(2,1)S(1)}, f32[128,32]{1,0:T(8,128)S(1)}, f32[8,128]{1,0:T(8,128)S(1)}) custom-call(bf16[4,128,128]{2,1,0:T(8,128)(2,1)} %pair.1, s32[4,128]{1,0:T(4,128)} %mask.1, bf16[2,128,512]{2,1,0:T(8,128)(2,1)} %pw.3, bf16[2,128,128]{2,1,0:T(8,128)(2,1)} %gw.3, ...), custom_call_target="tpu_custom_call" | custom-call | tf_op jit(solution)/shard_map/pallas_call | solution.py:154
  1.7 17.7 %all_to_all.20.sides = bf16[32,32,128]{2,1,0:T(8,128)(2,1)S(1)} all-to-all(bf16[32,32,128]{2,1,0:T(8,128)(2,1)S(1)} %get-tuple-element.13), channel_id=1, replica_groups=mesh['grp'=1,'row'=32,'ka'=1] {'row','ka'}, dimensions={0} | all-to-all | bytes 524288 | tf_op jit(solution)/shard_map/all_to_all | solution.py:165
  19.4 0.0 copy-start
  19.4 0.2 shard_map.101
  19.6 0.0 copy-start.1
  19.6 0.0 copy-start.2
  19.7 10.4 %all_to_all.21.summed = bf16[32,16,128]{2,1,0:T(8,128)(2,1)S(1)} all-to-all(bf16[32,16,128]{2,1,0:T(8,128)(2,1)S(1)} %shard_map.101), channel_id=1, replica_groups=mesh['grp'=1,'row'=32,'ka'=1] {'row','ka'}, dimensions={0} | all-to-all | bytes 262144 | tf_op jit(solution)/shard_map/all_to_all | solution.py:165
  30.1 0.0 copy-done
  30.1 0.0 copy-done.1
  30.1 0.0 copy-done.2
  30.1 0.8 %shard_map.102 = (bf16[32,32,128]{2,1,0:T(8,128)(2,1)S(1)}, f32[128,512]{1,0:T(8,128)S(1)}, bf16[128,512]{1,0:T(8,128)(2,1)S(1)}) custom-call(bf16[32,16,128]{2,1,0:T(8,128)(2,1)S(1)} %all_to_all.21.summed, bf16[128,512]{1,0:T(8,128)(2,1)S(1)} %get-tuple-element.14.old, f32[128,512]{1,0:T(8,128)S(1)} %get-tuple-element.15.old_gate, ...), custom_call_target="tpu_custom_call" | custom-call | tf_op jit(solution)/shard_map/pallas_call | solution.py:154
  30.9 12.4 %all_to_all.22.sides = bf16[32,32,128]{2,1,0:T(8,128)(2,1)S(1)} all-to-all(bf16[32,32,128]{2,1,0:T(8,128)(2,1)S(1)} %get-tuple-element.18), channel_id=1, replica_groups=mesh['grp'=1,'row'=32,'ka'=1] {'row','ka'}, dimensions={0} | all-to-all | bytes 524288 | tf_op jit(solution)/shard_map/all_to_all | solution.py:165
  43.3 0.2 shard_map.103
  43.5 10.4 %all_to_all.23.summed = bf16[32,16,128]{2,1,0:T(8,128)(2,1)S(1)} all-to-all(bf16[32,16,128]{2,1,0:T(8,128)(2,1)S(1)} %shard_map.103), channel_id=1, replica_groups=mesh['grp'=1,'row'=32,'ka'=1] {'row','ka'}, dimensions={0} | all-to-all | bytes 262144 | tf_op jit(solution)/shard_map/all_to_all | solution.py:165
  54.0 1.0 %shard_map.104 = bf16[4,128,128]{2,1,0:T(8,128)(2,1)} custom-call(bf16[32,16,128]{2,1,0:T(8,128)(2,1)S(1)} %all_to_all.23.summed, bf16[128,512]{1,0:T(8,128)(2,1)S(1)} %get-tuple-element.19.old, f32[128,512]{1,0:T(8,128)S(1)} %get-tuple-element.20.old_gate, f32[128,32]{1,0:T(8,128)S(1)} %get-tuple-element.16.columns, bf16[2,128,128]{2,1,0:T(8,128)(2,1)S(1)} %copy-done.2), custom_call_target="tpu_custom_call" | custom-call | tf_op jit(solution)/shard_map/pallas_call | solution.py:154
Async XLA Ops:
  19.4 10.7 %copy-start = (bf16[2,128,512]{2,1,0:T(8,128)(2,1)S(1)}, bf16[2,128,512]{2,1,0:T(8,128)(2,1)}, u32[]{:S(2)}) copy-start(bf16[2,128,512]{2,1,0:T(8,128)(2,1)} %pw.3) | copy-start | bytes 786436
  19.6 10.5 %copy-start.1 = (bf16[2,128,128]{2,1,0:T(8,128)(2,1)S(1)}, bf16[2,128,128]{2,1,0:T(8,128)(2,1)}, u32[]{:S(2)}) copy-start(bf16[2,128,128]{2,1,0:T(8,128)(2,1)} %gw.3) | copy-start | bytes 196612
  19.6 10.5 %copy-start.2 = (bf16[2,128,128]{2,1,0:T(8,128)(2,1)S(1)}, bf16[2,128,128]{2,1,0:T(8,128)(2,1)}, u32[]{:S(2)}) copy-start(bf16[2,128,128]{2,1,0:T(8,128)(2,1)} %ow.3) | copy-start | bytes 196612
where the time goes:
time: 55.2 us; the launch traced here: 55 us
  blocking collectives  51 us (92%)
  Pallas kernels  3.96 us (7%)
    all_to_all x4, blocking collectives, exchange(): lax.all_to_all(blocks, PEERS, split_axis=0, concat_axis=0, tiled=True)  51 us
    pallas_call x5, Pallas kernels, call(): pl.pallas_call(kernel, out_shape=[jax.ShapeDtypeStruct(*o) for o in outs]...  3.96 us

commit v1 on v0

--- a/solution.py
+++ b/solution.py
@@ -51,6 +51,43 @@
         blocks.append(jnp.where(low, even, down).reshape(count * 4, width))
         blocks.append(jnp.where(low, up, odd).reshape(count * 4, width))
     return blocks
+
+
+def place():
+    index = lax.axis_index("row")
+    return index >> 3, (index >> 1) & 3, index & 1
+
+
+def device(z, chip, core):
+    return z * 8 + chip * 2 + core
+
+
+def arrived_blocks(me, near, far):
+    z, chip, core = me
+    for m in range(4):
+        for n in range(4):
+            yield (z ^ n, chip ^ m, core), near[m][core, n]
+            yield (z ^ n, chip ^ m, core ^ 1), far[m, n]
+
+
+def to_planes(blocks, outs):
+    z, _, _ = place()
+    for m in range(4):
+        outs[m][...] = blocks[pl.ds(pl.multiple_of((z ^ m) * 8, 8), 8)]
+
+
+def to_chips_kernel(z0, z1, z2, z3, *outs):
+    _, chip, _ = place()
+    for m in range(4):
+        for n, came in enumerate((z0, z1, z2, z3)):
+            for core in range(2):
+                outs[m][core, n] = came[(chip ^ m) * 2 + core]
+
+
+def to_core_kernel(c0, c1, c2, c3, out):
+    _, _, core = place()
+    for m, came in enumerate((c0, c1, c2, c3)):
+        out[m] = came[core ^ 1]
 
 
 def sigmoid(x):
@@ -83,11 +120,13 @@
     send[:, 16:32, :] = mixed[1].reshape(rows // 16, 16, width).astype(BF16)
 
 
-def finish(u, z, summed, gate, out_weight, columns, mixed):
+def finish(u, z, near, far, gate, out_weight, columns, mixed):
     width = z[0].shape[1]
     gain, offset, bias = broadcast_columns(columns, u * EACH + 7, 3, width)
     turned = out_weight.T
-    mixed[...] = summed[...].astype(F32).reshape(mixed.shape)
+    me = place()
+    for at, block in arrived_blocks(me, near, far):
+        mixed[pl.ds(pl.multiple_of(device(*at) * 16, 16), 16), :] = block.astype(F32)
     results = []
     for pair in range(0, OWN, 2):
         blocks = [mixed[pl.ds(i, mixed.shape[0] // OWN, stride=OWN), :] for i in (pair, pair + 1)]
@@ -128,25 +167,26 @@
     project(0, [v.astype(F32) for v in z], keep, pw_in[...], gw_in[...], columns, send, gate, mixed)
 
 
-def middle_kernel(summed, old, old_gate, columns, keep, pw, gw, ow, send, gate, turned, mixed, mixed_back):
+def middle_kernel(c0, c1, c2, c3, far, old, old_gate, columns, keep, pw, gw, ow, send, gate, turned, mixed, mixed_back):
     width = keep.shape[1]
-    z = finish(0, [old[:, i * width : (i + 1) * width] for i in range(OWN)], summed, old_gate, ow[0], columns, mixed_back)
+    z = finish(0, [old[:, i * width : (i + 1) * width] for i in range(OWN)], (c0, c1, c2, c3), far, old_gate, ow[0], columns, mixed_back)
     for i in range(OWN):
         turned[:, i * width : (i + 1) * width] = z[i]
     project(1, [v.astype(F32) for v in z], keep, pw[1], gw[1], columns, send, gate, mixed)
 
 
-def last_kernel(summed, old, old_gate, columns, ow, out, mixed_back):
+def last_kernel(c0, c1, c2, c3, far, old, old_gate, columns, ow, out, mixed_back):
     width = out.shape[1]
-    z = finish(1, [old[:, i * width : (i + 1) * width] for i in range(OWN)], summed, old_gate, ow[1], columns, mixed_back)
+    z = finish(1, [old[:, i * width : (i + 1) * width] for i in range(OWN)], (c0, c1, c2, c3), far, old_gate, ow[1], columns, mixed_back)
     for i in range(OWN):
         out[i] = z[i].T
 
 
-def triangle_kernel(incoming, sides, out):
+def triangle_kernel(incoming, sides, p0, p1, p2, p3, summed):
     left, right = [unpack(sides[:, n : n + 16, :].astype(F32)) for n in (0, 16)]
     product = over_rows if incoming else over_columns
-    out[...] = pack([product(a.astype(BF16), b.astype(BF16)) for a, b in zip(left, right)]).astype(BF16)
+    summed[...] = pack([product(a.astype(BF16), b.astype(BF16)) for a, b in zip(left, right)]).astype(BF16)
+    to_planes(summed, (p0, p1, p2, p3))
 
 
 def call(kernel, outs, scratch, *args, place=pltpu.VMEM):
@@ -165,11 +205,25 @@
     return lax.all_to_all(blocks, PEERS, split_axis=0, concat_axis=0, tiled=True)
 
 
+def permute(values, change):
+    return lax.ppermute(values, "row", [(d, d ^ change) for d in range(32)])
+
+
+def triangle(incoming, sides):
+    width = sides.shape[2]
+    whole = pltpu.VMEM((32, 16, width), BF16)
+    planes = call(functools.partial(triangle_kernel, incoming), [((8, 16, width), BF16)] * 4, [whole], sides)
+    planes = [permute(v, n << 3) if n else v for n, v in enumerate(planes)]
+    chips = call(to_chips_kernel, [((2, 4, 16, width), BF16)] * 4, [], *planes)
+    chips = [permute(v, n << 1) if n else v for n, v in enumerate(chips)]
+    (cores,) = call(to_core_kernel, [((4, 4, 16, width), BF16)], [], *chips)
+    return *chips, permute(cores, 1)
+
+
 def packed_updates(count, pair_rep, pair_mask, pw, pb, gw, gb, ow, ob, ns, no):
     rows_of, width, channels = pair_rep.shape
     flat = (channels, rows_of * width)
     projected = [((count, 32, width), BF16), (flat, F32), (flat, BF16)]
-    summed = [((count, 16, width), BF16)]
     params = [pair_rep, pair_mask, pw, gw, pb, gb, ob, ns, no]
     params = [pltpu.with_memory_space_constraint(v, pltpu.HBM) for v in params]
     held = [pltpu.VMEM(v.shape[1:] if n in (2, 3) else v.shape, v.dtype) for n, v in enumerate(params)]
@@ -178,10 +232,10 @@
     mixed = pltpu.VMEM((2, OWN * channels, width), F32)
     kept = [((channels, 2 * EACH), F32), ((2 * OWN, width), F32)]
     send, gate, turned, columns, keep = call(first_kernel, projected + kept, held + [mixed], *params, place=pltpu.HBM)
-    (send,) = call(functools.partial(triangle_kernel, False), summed, [], exchange(send))
-    send, gate, turned = call(middle_kernel, projected, [mixed, back], exchange(send), turned, gate, columns, keep, pw, gw, ow)
-    (send,) = call(functools.partial(triangle_kernel, True), summed, [], exchange(send))
-    (out,) = call(last_kernel, [(pair_rep.shape, BF16)], [back], exchange(send), turned, gate, columns, ow)
+    sums = triangle(False, exchange(send))
+    send, gate, turned = call(middle_kernel, projected, [mixed, back], *sums, turned, gate, columns, keep, pw, gw, ow)
+    sums = triangle(True, exchange(send))
+    (out,) = call(last_kernel, [(pair_rep.shape, BF16)], [back], *sums, turned, gate, columns, ow)
     return out
 
 
@@ -225,7 +279,7 @@
     def on_device(pair_rep, pair_mask, *params):
         rows_of, width, channels = pair_rep.shape
         hidden = params[0].shape[2] // 4
-        fits = peers[1] == 1 and rows_of == OWN and hidden == OWN * count and count % 2 == 0
+        fits = peers[1] == 1 and rows_of == OWN and hidden == OWN * count and count == 32
         if fits and channels == hidden == 128 and width % 128 == 0:
             return packed_updates(count, pair_rep, pair_mask, *params)
         return plain_updates(peers, pair_rep, pair_mask, *params)

time: 55.2 us -> 67.7 us (1.23)
  blocking collectives: 51 us -> 32.1 us
  starting transfers between devices: 0 us -> 16.1 us
  waiting for transfers between devices: 0 us -> 15.2 us
    all_to_all x4 -> x2, blocking collectives: 51 us -> 32.1 us  [exchange(): lax.all_to_all(blocks, PEERS, split_axis=0, concat_axis=0, tiled=True)]
    ppermute x0 -> x14, starting transfers between devices: none -> 16.1 us  [permute(): return lax.ppermute(values, 'row', [(d, d ^ change) for d in range(32)])]
    ppermute x0 -> x14, waiting for transfers between devices: none -> 15.2 us  [permute(): return lax.ppermute(values, 'row', [(d, d ^ change) for d in range(32)])]
    pallas_call x5 -> x9, Pallas kernels: 3.96 us -> 4.04 us  [call(): pl.pallas_call(kernel, out_shape=[jax.ShapeDtypeStruct(*o) for o in outs]...]
  transfers between devices with their start and end apart: 0 -> 14, of which waited for: 0 -> 12; matrix products, arithmetic and copies ran while one was open for 0% -> 0% of each run, Pallas kernels for 0% -> 0%
where the time goes in v1:
time: 67.7 us; the launch traced here: 67.5 us
  blocking collectives  32.1 us (47%)
  starting transfers between devices  16.1 us (24%)
  waiting for transfers between devices  15.2 us (22%)
  Pallas kernels  4.04 us (6%)
    all_to_all x2, blocking collectives, exchange(): lax.all_to_all(blocks, PEERS, split_axis=0, concat_axis=0, tiled=True)  32.1 us
    ppermute x14, starting transfers between devices, permute(): return lax.ppermute(values, 'row', [(d, d ^ change) for d in range(32)])  16.1 us
    ppermute x14, waiting for transfers between devices, permute(): return lax.ppermute(values, 'row', [(d, d ^ change) for d in range(32)])  15.2 us
    pallas_call x9, Pallas kernels, call(): pl.pallas_call(kernel, out_shape=[jax.ShapeDtypeStruct(*o) for o in outs]...  4.04 us
  transfers between devices with their start and end apart: 14, of which 12 were waited for; matrix products, arithmetic and copies ran while one was open for 0% of the time, Pallas kernels for 0%

profile of v1, /device:TPU:0, one launch (start us, length us, event | category | flops | bytes accessed | tf_op | source)
XLA Modules:
  0.0 67.5 jit_solution(2201836591532583294)
XLA Ops:
  0.0 1.7 %shard_map.100 = (bf16[32,32,128]{2,1,0:T(8,128)(2,1)S(1)}, f32[128,512]{1,0:T(8,128)S(1)}, bf16[128,512]{1,0:T(8,128)(2,1)S(1)}, f32[128,32]{1,0:T(8,128)S(1)}, f32[8,128]{1,0:T(8,128)S(1)}) custom-call(bf16[4,128,128]{2,1,0:T(8,128)(2,1)} %pair.1, s32[4,128]{1,0:T(4,128)} %mask.1, bf16[2,128,512]{2,1,0:T(8,128)(2,1)} %pw.3, bf16[2,128,128]{2,1,0:T(8,128)(2,1)} %gw.3, ...), custom_call_target="tpu_custom_call" | custom-call | tf_op jit(solution)/shard_map/pallas_call | solution.py:194
  1.7 17.7 %all_to_all.10.sides = bf16[32,32,128]{2,1,0:T(8,128)(2,1)S(1)} all-to-all(bf16[32,32,128]{2,1,0:T(8,128)(2,1)S(1)} %get-tuple-element.29), channel_id=1, replica_groups=mesh['grp'=1,'row'=32,'ka'=1] {'row','ka'}, dimensions={0} | all-to-all | bytes 524288 | tf_op jit(solution)/shard_map/all_to_all | solution.py:205
  19.4 0.0 copy-start
  19.4 0.2 shard_map.101
  19.6 1.0 %collective-permute-start = (bf16[8,16,128]{2,1,0:T(8,128)(2,1)S(1)}, bf16[8,16,128]{2,1,0:T(8,128)(2,1)S(1)}, u32[]{:S(2)}, u32[]{:S(2)}) collective-permute-start(bf16[8,16,128]{2,1,0:T(8,128)(2,1)S(1)} %get-tuple-element.31), channel_id=1, source_target_pairs={{0,8},{1,9},{2,10},{3,11},{4,12},{5,13},{6,14},{7,15},{8,0},{9,1},... | collective-permute-start | bytes 98312 | tf_op jit(solution)/shard_map/ppermute | solution.py:209
  20.6 1.0 %collective-permute-start.1 = (bf16[8,16,128]{2,1,0:T(8,128)(2,1)S(1)}, bf16[8,16,128]{2,1,0:T(8,128)(2,1)S(1)}, u32[]{:S(2)}, u32[]{:S(2)}) collective-permute-start(bf16[8,16,128]{2,1,0:T(8,128)(2,1)S(1)} %get-tuple-element.32), channel_id=1, source_target_pairs={{0,16},{1,17},{2,18},{3,19},{4,20},{5,21},{6,22},{7,23},{8,24},{9,... | collective-permute-start | bytes 98312 | tf_op jit(solution)/shard_map/ppermute | solution.py:209
  21.6 2.5 %collective-permute-start.2 = (bf16[8,16,128]{2,1,0:T(8,128)(2,1)S(1)}, bf16[8,16,128]{2,1,0:T(8,128)(2,1)S(1)}, u32[]{:S(2)}, u32[]{:S(2)}) collective-permute-start(bf16[8,16,128]{2,1,0:T(8,128)(2,1)S(1)} %get-tuple-element.33), channel_id=1, source_target_pairs={{0,24},{1,25},{2,26},{3,27},{4,28},{5,29},{6,30},{7,31},{8,16},{9,... | collective-permute-start | bytes 98312 | tf_op jit(solution)/shard_map/ppermute | solution.py:209
  24.1 0.0 collective-permute-done.z1
  24.1 2.0 %collective-permute-done.1.z2 = bf16[8,16,128]{2,1,0:T(8,128)(2,1)S(1)} collective-permute-done((bf16[8,16,128]{2,1,0:T(8,128)(2,1)S(1)}, bf16[8,16,128]{2,1,0:T(8,128)(2,1)S(1)}, u32[]{:S(2)}, u32[]{:S(2)}) %collective-permute-start.1) | collective-permute-done | bytes 32800 | tf_op jit(solution)/shard_map/ppermute | solution.py:209
  26.1 1.2 %collective-permute-done.2.z3 = bf16[8,16,128]{2,1,0:T(8,128)(2,1)S(1)} collective-permute-done((bf16[8,16,128]{2,1,0:T(8,128)(2,1)S(1)}, bf16[8,16,128]{2,1,0:T(8,128)(2,1)S(1)}, u32[]{:S(2)}, u32[]{:S(2)}) %collective-permute-start.2) | collective-permute-done | bytes 32800 | tf_op jit(solution)/shard_map/ppermute | solution.py:209
  27.3 0.6 collective-permute-start.3
  28.0 1.3 %collective-permute-start.4 = (bf16[2,4,16,128]{3,2,1,0:T(8,128)(2,1)S(1)}, bf16[2,4,16,128]{3,2,1,0:T(8,128)(2,1)S(1)}, u32[]{:S(2)}, u32[]{:S(2)}) collective-permute-start(bf16[2,4,16,128]{3,2,1,0:T(8,128)(2,1)S(1)} %get-tuple-element.36), channel_id=1, source_target_pairs={{0,4},{1,5},{2,6},{3,7},{4,0},{5,1},{6,2},{7,3},{8,12},{9,13},{10,... | collective-permute-start | bytes 98312 | tf_op jit(solution)/shard_map/ppermute | solution.py:209
  29.2 1.7 %collective-permute-start.5 = (bf16[2,4,16,128]{3,2,1,0:T(8,128)(2,1)S(1)}, bf16[2,4,16,128]{3,2,1,0:T(8,128)(2,1)S(1)}, u32[]{:S(2)}, u32[]{:S(2)}) collective-permute-start(bf16[2,4,16,128]{3,2,1,0:T(8,128)(2,1)S(1)} %get-tuple-element.37), channel_id=1, source_target_pairs={{0,6},{1,7},{2,4},{3,5},{4,2},{5,3},{6,0},{7,1},{8,14},{9,15},{10,... | collective-permute-start | bytes 98312 | tf_op jit(solution)/shard_map/ppermute | solution.py:209
  30.9 0.4 collective-permute-done.3.c1
  31.3 0.6 collective-permute-done.4.c2
  31.9 2.2 %collective-permute-done.5.c3 = bf16[2,4,16,128]{3,2,1,0:T(8,128)(2,1)S(1)} collective-permute-done((bf16[2,4,16,128]{3,2,1,0:T(8,128)(2,1)S(1)}, bf16[2,4,16,128]{3,2,1,0:T(8,128)(2,1)S(1)}, u32[]{:S(2)}, u32[]{:S(2)}) %collective-permute-start.5) | collective-permute-done | bytes 32800 | tf_op jit(solution)/shard_map/ppermute | solution.py:209
  34.1 0.0 copy-start.1
  34.1 0.0 copy-start.2
  34.1 0.1 collective-permute-start.6
  34.1 1.2 %collective-permute-done.6.far = bf16[4,4,16,128]{3,2,1,0:T(8,128)(2,1)S(1)} collective-permute-done((bf16[4,4,16,128]{3,2,1,0:T(8,128)(2,1)S(1)}, bf16[4,4,16,128]{3,2,1,0:T(8,128)(2,1)S(1)}, u32[]{:S(2)}, u32[]{:S(2)}) %collective-permute-start.6) | collective-permute-done | bytes 65568 | tf_op jit(solution)/shard_map/ppermute | solution.py:209
  35.4 0.0 copy-done
  35.4 0.0 copy-done.1
  35.4 0.0 copy-done.2
  35.4 0.8 %shard_map.104 = (bf16[32,32,128]{2,1,0:T(8,128)(2,1)S(1)}, f32[128,512]{1,0:T(8,128)S(1)}, bf16[128,512]{1,0:T(8,128)(2,1)S(1)}) custom-call(bf16[2,4,16,128]{3,2,1,0:T(8,128)(2,1)S(1)} %get-tuple-element.34.c0, bf16[2,4,16,128]{3,2,1,0:T(8,128)(2,1)S(1)} %collective-permute-done.3.c1, bf16[2,4,16,128]{3,2,1,0:T(8,128)(2,1)S(1)} %collective-permute-done.4.c2, ...), custom_call_target="tpu_custom_call" | custom-call | tf_op jit(solution)/shard_map/pallas_call | solution.py:194
  36.2 14.4 %all_to_all.11.sides = bf16[32,32,128]{2,1,0:T(8,128)(2,1)S(1)} all-to-all(bf16[32,32,128]{2,1,0:T(8,128)(2,1)S(1)} %get-tuple-element.42), channel_id=1, replica_groups=mesh['grp'=1,'row'=32,'ka'=1] {'row','ka'}, dimensions={0} | all-to-all | bytes 524288 | tf_op jit(solution)/shard_map/all_to_all | solution.py:205
  50.6 0.2 shard_map.105
  50.8 1.0 %collective-permute-start.7 = (bf16[8,16,128]{2,1,0:T(8,128)(2,1)S(1)}, bf16[8,16,128]{2,1,0:T(8,128)(2,1)S(1)}, u32[]{:S(2)}, u32[]{:S(2)}) collective-permute-start(bf16[8,16,128]{2,1,0:T(8,128)(2,1)S(1)} %get-tuple-element.44), channel_id=1, source_target_pairs={{0,8},{1,9},{2,10},{3,11},{4,12},{5,13},{6,14},{7,15},{8,0},{9,1},... | collective-permute-start | bytes 98312 | tf_op jit(solution)/shard_map/ppermute | solution.py:209
  51.8 1.0 %collective-permute-start.8 = (bf16[8,16,128]{2,1,0:T(8,128)(2,1)S(1)}, bf16[8,16,128]{2,1,0:T(8,128)(2,1)S(1)}, u32[]{:S(2)}, u32[]{:S(2)}) collective-permute-start(bf16[8,16,128]{2,1,0:T(8,128)(2,1)S(1)} %get-tuple-element.45), channel_id=1, source_target_pairs={{0,16},{1,17},{2,18},{3,19},{4,20},{5,21},{6,22},{7,23},{8,24},{9,... | collective-permute-start | bytes 98312 | tf_op jit(solution)/shard_map/ppermute | solution.py:209
  52.8 2.5 %collective-permute-start.9 = (bf16[8,16,128]{2,1,0:T(8,128)(2,1)S(1)}, bf16[8,16,128]{2,1,0:T(8,128)(2,1)S(1)}, u32[]{:S(2)}, u32[]{:S(2)}) collective-permute-start(bf16[8,16,128]{2,1,0:T(8,128)(2,1)S(1)} %get-tuple-element.46), channel_id=1, source_target_pairs={{0,24},{1,25},{2,26},{3,27},{4,28},{5,29},{6,30},{7,31},{8,16},{9,... | collective-permute-start | bytes 98312 | tf_op jit(solution)/shard_map/ppermute | solution.py:209
  55.3 0.0 collective-permute-done.7.z1
  55.3 2.0 %collective-permute-done.8.z2 = bf16[8,16,128]{2,1,0:T(8,128)(2,1)S(1)} collective-permute-done((bf16[8,16,128]{2,1,0:T(8,128)(2,1)S(1)}, bf16[8,16,128]{2,1,0:T(8,128)(2,1)S(1)}, u32[]{:S(2)}, u32[]{:S(2)}) %collective-permute-start.8) | collective-permute-done | bytes 32800 | tf_op jit(solution)/shard_map/ppermute | solution.py:209
  57.3 1.2 %collective-permute-done.9.z3 = bf16[8,16,128]{2,1,0:T(8,128)(2,1)S(1)} collective-permute-done((bf16[8,16,128]{2,1,0:T(8,128)(2,1)S(1)}, bf16[8,16,128]{2,1,0:T(8,128)(2,1)S(1)}, u32[]{:S(2)}, u32[]{:S(2)}) %collective-permute-start.9) | collective-permute-done | bytes 32800 | tf_op jit(solution)/shard_map/ppermute | solution.py:209
  58.5 0.6 collective-permute-start.10
  59.1 1.3 %collective-permute-start.11 = (bf16[2,4,16,128]{3,2,1,0:T(8,128)(2,1)S(1)}, bf16[2,4,16,128]{3,2,1,0:T(8,128)(2,1)S(1)}, u32[]{:S(2)}, u32[]{:S(2)}) collective-permute-start(bf16[2,4,16,128]{3,2,1,0:T(8,128)(2,1)S(1)} %get-tuple-element.49), channel_id=1, source_target_pairs={{0,4},{1,5},{2,6},{3,7},{4,0},{5,1},{6,2},{7,3},{8,12},{9,13},{10,... | collective-permute-start | bytes 98312 | tf_op jit(solution)/shard_map/ppermute | solution.py:209
  60.4 1.7 %collective-permute-start.12 = (bf16[2,4,16,128]{3,2,1,0:T(8,128)(2,1)S(1)}, bf16[2,4,16,128]{3,2,1,0:T(8,128)(2,1)S(1)}, u32[]{:S(2)}, u32[]{:S(2)}) collective-permute-start(bf16[2,4,16,128]{3,2,1,0:T(8,128)(2,1)S(1)} %get-tuple-element.50), channel_id=1, source_target_pairs={{0,6},{1,7},{2,4},{3,5},{4,2},{5,3},{6,0},{7,1},{8,14},{9,15},{10,... | collective-permute-start | bytes 98312 | tf_op jit(solution)/shard_map/ppermute | solution.py:209
  62.1 0.4 collective-permute-done.10.c1
  62.5 0.6 collective-permute-done.11.c2
  63.1 2.2 %collective-permute-done.12.c3 = bf16[2,4,16,128]{3,2,1,0:T(8,128)(2,1)S(1)} collective-permute-done((bf16[2,4,16,128]{3,2,1,0:T(8,128)(2,1)S(1)}, bf16[2,4,16,128]{3,2,1,0:T(8,128)(2,1)S(1)}, u32[]{:S(2)}, u32[]{:S(2)}) %collective-permute-start.12) | collective-permute-done | bytes 32800 | tf_op jit(solution)/shard_map/ppermute | solution.py:209
  65.2 0.0 collective-permute-start.13
  65.2 1.2 %collective-permute-done.13.far = bf16[4,4,16,128]{3,2,1,0:T(8,128)(2,1)S(1)} collective-permute-done((bf16[4,4,16,128]{3,2,1,0:T(8,128)(2,1)S(1)}, bf16[4,4,16,128]{3,2,1,0:T(8,128)(2,1)S(1)}, u32[]{:S(2)}, u32[]{:S(2)}) %collective-permute-start.13) | collective-permute-done | bytes 65568 | tf_op jit(solution)/shard_map/ppermute | solution.py:209
  66.5 1.0 %shard_map.108 = bf16[4,128,128]{2,1,0:T(8,128)(2,1)} custom-call(bf16[2,4,16,128]{3,2,1,0:T(8,128)(2,1)S(1)} %get-tuple-element.47.c0, bf16[2,4,16,128]{3,2,1,0:T(8,128)(2,1)S(1)} %collective-permute-done.10.c1, bf16[2,4,16,128]{3,2,1,0:T(8,128)(2,1)S(1)} %collective-permute-done.11.c2, bf16[2,4,16,128]{3,2,1,0:T(8,128)(2,1)S(1)} %collective-permute-done.12.c3, ...), custom_call_target="tpu_custom_call" | custom-call | tf_op jit(solution)/shard_map/pallas_call | solution.py:194
  (4 shorter events, 0.0 us)
Async XLA Ops:
  19.4 16.0 %copy-start = (bf16[2,128,512]{2,1,0:T(8,128)(2,1)S(1)}, bf16[2,128,512]{2,1,0:T(8,128)(2,1)}, u32[]{:S(2)}) copy-start(bf16[2,128,512]{2,1,0:T(8,128)(2,1)} %pw.3) | copy-start | bytes 786436
  19.6 4.5 %collective-permute-start = (bf16[8,16,128]{2,1,0:T(8,128)(2,1)S(1)}, bf16[8,16,128]{2,1,0:T(8,128)(2,1)S(1)}, u32[]{:S(2)}, u32[]{:S(2)}) collective-permute-start(bf16[8,16,128]{2,1,0:T(8,128)(2,1)S(1)} %get-tuple-element.31), channel_id=1, source_target_pairs={{0,8},{1,9},{2,10},{3,11},{4,12},{5,13},{6,14},{7,15},{8,0},{9,1},... | collective-permute-start | bytes 98312 | tf_op jit(solution)/shard_map/ppermute | solution.py:209
  20.6 5.5 %collective-permute-start.1 = (bf16[8,16,128]{2,1,0:T(8,128)(2,1)S(1)}, bf16[8,16,128]{2,1,0:T(8,128)(2,1)S(1)}, u32[]{:S(2)}, u32[]{:S(2)}) collective-permute-start(bf16[8,16,128]{2,1,0:T(8,128)(2,1)S(1)} %get-tuple-element.32), channel_id=1, source_target_pairs={{0,16},{1,17},{2,18},{3,19},{4,20},{5,21},{6,22},{7,23},{8,24},{9,... | collective-permute-start | bytes 98312 | tf_op jit(solution)/shard_map/ppermute | solution.py:209
  21.6 5.7 %collective-permute-start.2 = (bf16[8,16,128]{2,1,0:T(8,128)(2,1)S(1)}, bf16[8,16,128]{2,1,0:T(8,128)(2,1)S(1)}, u32[]{:S(2)}, u32[]{:S(2)}) collective-permute-start(bf16[8,16,128]{2,1,0:T(8,128)(2,1)S(1)} %get-tuple-element.33), channel_id=1, source_target_pairs={{0,24},{1,25},{2,26},{3,27},{4,28},{5,29},{6,30},{7,31},{8,16},{9,... | collective-permute-start | bytes 98312 | tf_op jit(solution)/shard_map/ppermute | solution.py:209
  27.3 4.0 %collective-permute-start.3 = (bf16[2,4,16,128]{3,2,1,0:T(8,128)(2,1)S(1)}, bf16[2,4,16,128]{3,2,1,0:T(8,128)(2,1)S(1)}, u32[]{:S(2)}, u32[]{:S(2)}) collective-permute-start(bf16[2,4,16,128]{3,2,1,0:T(8,128)(2,1)S(1)} %get-tuple-element.35), channel_id=1, source_target_pairs={{0,2},{1,3},{2,0},{3,1},{4,6},{5,7},{6,4},{7,5},{8,10},{9,11},{10,... | collective-permute-start | bytes 98312 | tf_op jit(solution)/shard_map/ppermute | solution.py:209
  28.0 3.9 %collective-permute-start.4 = (bf16[2,4,16,128]{3,2,1,0:T(8,128)(2,1)S(1)}, bf16[2,4,16,128]{3,2,1,0:T(8,128)(2,1)S(1)}, u32[]{:S(2)}, u32[]{:S(2)}) collective-permute-start(bf16[2,4,16,128]{3,2,1,0:T(8,128)(2,1)S(1)} %get-tuple-element.36), channel_id=1, source_target_pairs={{0,4},{1,5},{2,6},{3,7},{4,0},{5,1},{6,2},{7,3},{8,12},{9,13},{10,... | collective-permute-start | bytes 98312 | tf_op jit(solution)/shard_map/ppermute | solution.py:209
  29.2 4.8 %collective-permute-start.5 = (bf16[2,4,16,128]{3,2,1,0:T(8,128)(2,1)S(1)}, bf16[2,4,16,128]{3,2,1,0:T(8,128)(2,1)S(1)}, u32[]{:S(2)}, u32[]{:S(2)}) collective-permute-start(bf16[2,4,16,128]{3,2,1,0:T(8,128)(2,1)S(1)} %get-tuple-element.37), channel_id=1, source_target_pairs={{0,6},{1,7},{2,4},{3,5},{4,2},{5,3},{6,0},{7,1},{8,14},{9,15},{10,... | collective-permute-start | bytes 98312 | tf_op jit(solution)/shard_map/ppermute | solution.py:209
  34.1 1.3 %copy-start.1 = (bf16[2,128,128]{2,1,0:T(8,128)(2,1)S(1)}, bf16[2,128,128]{2,1,0:T(8,128)(2,1)}, u32[]{:S(2)}) copy-start(bf16[2,128,128]{2,1,0:T(8,128)(2,1)} %gw.3) | copy-start | bytes 196612
  34.1 1.3 %copy-start.2 = (bf16[2,128,128]{2,1,0:T(8,128)(2,1)S(1)}, bf16[2,128,128]{2,1,0:T(8,128)(2,1)}, u32[]{:S(2)}) copy-start(bf16[2,128,128]{2,1,0:T(8,128)(2,1)} %ow.3) | copy-start | bytes 196612
  34.1 1.3 %collective-permute-start.6 = (bf16[4,4,16,128]{3,2,1,0:T(8,128)(2,1)S(1)}, bf16[4,4,16,128]{3,2,1,0:T(8,128)(2,1)S(1)}, u32[]{:S(2)}, u32[]{:S(2)}) collective-permute-start(bf16[4,4,16,128]{3,2,1,0:T(8,128)(2,1)S(1)} %shard_map.103), channel_id=1, source_target_pairs={{0,1},{1,0},{2,3},{3,2},{4,5},{5,4},{6,7},{7,6},{8,9},{9,8},{10,11... | collective-permute-start | bytes 196616 | tf_op jit(solution)/shard_map/ppermute | solution.py:209
  50.8 4.5 %collective-permute-start.7 = (bf16[8,16,128]{2,1,0:T(8,128)(2,1)S(1)}, bf16[8,16,128]{2,1,0:T(8,128)(2,1)S(1)}, u32[]{:S(2)}, u32[]{:S(2)}) collective-permute-start(bf16[8,16,128]{2,1,0:T(8,128)(2,1)S(1)} %get-tuple-element.44), channel_id=1, source_target_pairs={{0,8},{1,9},{2,10},{3,11},{4,12},{5,13},{6,14},{7,15},{8,0},{9,1},... | collective-permute-start | bytes 98312 | tf_op jit(solution)/shard_map/ppermute | solution.py:209
  51.8 5.5 %collective-permute-start.8 = (bf16[8,16,128]{2,1,0:T(8,128)(2,1)S(1)}, bf16[8,16,128]{2,1,0:T(8,128)(2,1)S(1)}, u32[]{:S(2)}, u32[]{:S(2)}) collective-permute-start(bf16[8,16,128]{2,1,0:T(8,128)(2,1)S(1)} %get-tuple-element.45), channel_id=1, source_target_pairs={{0,16},{1,17},{2,18},{3,19},{4,20},{5,21},{6,22},{7,23},{8,24},{9,... | collective-permute-start | bytes 98312 | tf_op jit(solution)/shard_map/ppermute | solution.py:209
  52.8 5.7 %collective-permute-start.9 = (bf16[8,16,128]{2,1,0:T(8,128)(2,1)S(1)}, bf16[8,16,128]{2,1,0:T(8,128)(2,1)S(1)}, u32[]{:S(2)}, u32[]{:S(2)}) collective-permute-start(bf16[8,16,128]{2,1,0:T(8,128)(2,1)S(1)} %get-tuple-element.46), channel_id=1, source_target_pairs={{0,24},{1,25},{2,26},{3,27},{4,28},{5,29},{6,30},{7,31},{8,16},{9,... | collective-permute-start | bytes 98312 | tf_op jit(solution)/shard_map/ppermute | solution.py:209
  58.5 4.0 %collective-permute-start.10 = (bf16[2,4,16,128]{3,2,1,0:T(8,128)(2,1)S(1)}, bf16[2,4,16,128]{3,2,1,0:T(8,128)(2,1)S(1)}, u32[]{:S(2)}, u32[]{:S(2)}) collective-permute-start(bf16[2,4,16,128]{3,2,1,0:T(8,128)(2,1)S(1)} %get-tuple-element.48), channel_id=1, source_target_pairs={{0,2},{1,3},{2,0},{3,1},{4,6},{5,7},{6,4},{7,5},{8,10},{9,11},{10,... | collective-permute-start | bytes 98312 | tf_op jit(solution)/shard_map/ppermute | solution.py:209
  59.1 3.9 %collective-permute-start.11 = (bf16[2,4,16,128]{3,2,1,0:T(8,128)(2,1)S(1)}, bf16[2,4,16,128]{3,2,1,0:T(8,128)(2,1)S(1)}, u32[]{:S(2)}, u32[]{:S(2)}) collective-permute-start(bf16[2,4,16,128]{3,2,1,0:T(8,128)(2,1)S(1)} %get-tuple-element.49), channel_id=1, source_target_pairs={{0,4},{1,5},{2,6},{3,7},{4,0},{5,1},{6,2},{7,3},{8,12},{9,13},{10,... | collective-permute-start | bytes 98312 | tf_op jit(solution)/shard_map/ppermute | solution.py:209
  60.4 4.8 %collective-permute-start.12 = (bf16[2,4,16,128]{3,2,1,0:T(8,128)(2,1)S(1)}, bf16[2,4,16,128]{3,2,1,0:T(8,128)(2,1)S(1)}, u32[]{:S(2)}, u32[]{:S(2)}) collective-permute-start(bf16[2,4,16,128]{3,2,1,0:T(8,128)(2,1)S(1)} %get-tuple-element.50), channel_id=1, source_target_pairs={{0,6},{1,7},{2,4},{3,5},{4,2},{5,3},{6,0},{7,1},{8,14},{9,15},{10,... | collective-permute-start | bytes 98312 | tf_op jit(solution)/shard_map/ppermute | solution.py:209
  65.2 1.3 %collective-permute-start.13 = (bf16[4,4,16,128]{3,2,1,0:T(8,128)(2,1)S(1)}, bf16[4,4,16,128]{3,2,1,0:T(8,128)(2,1)S(1)}, u32[]{:S(2)}, u32[]{:S(2)}) collective-permute-start(bf16[4,4,16,128]{3,2,1,0:T(8,128)(2,1)S(1)} %shard_map.107), channel_id=1, source_target_pairs={{0,1},{1,0},{2,3},{3,2},{4,5},{5,4},{6,7},{7,6},{8,9},{9,8},{10,11... | collective-permute-start | bytes 196616 | tf_op jit(solution)/shard_map/ppermute | solution.py:209

commit v2 on v0

--- a/solution.py
+++ b/solution.py
@@ -21,11 +21,15 @@
     return lax.dot_general(a, b, (((1,), (1,)), ((), ())), preferred_element_type=F32)
 
 
-def layer_norm(values, norm_gain, norm_bias):
+def standardised(values):
     average = jnp.mean(values, 0, keepdims=True)
     centred = values - average
     variance = jnp.mean(centred * centred, 0, keepdims=True)
-    return centred * lax.rsqrt(variance + 1e-05) * norm_gain + norm_bias
+    return centred * lax.rsqrt(variance + 1e-05)
+
+
+def layer_norm(values, norm_gain, norm_bias):
+    return standardised(values) * norm_gain + norm_bias
 
 
 def pack(blocks):
@@ -62,31 +66,27 @@
     return [jnp.broadcast_to(held[:, n : n + 1], (held.shape[0], width)) for n in range(first, first + many)]
 
 
-def project(u, z, mask, proj_weight, gate_weight, columns, send, gate, mixed):
-    width = z[0].shape[1]
+def project(u, norm, mask, proj_weight, columns, send, mixed):
+    width = norm.shape[1] // OWN
     h = proj_weight.shape[1] // 4
     rows = mixed.shape[1]
-    gain, offset, *biases = broadcast_columns(columns, u * EACH, 7, width)
-    turned = [proj_weight[:, n * h : (n + 1) * h].T for n in range(4)] + [gate_weight.T]
-    for pair in range(0, OWN, 2):
-        normed = [layer_norm(z[i], gain, offset).astype(BF16) for i in (pair, pair + 1)]
-        normed = jnp.concatenate(normed, 1)
-        both = [jnp.dot(w, normed, preferred_element_type=F32) for w in turned]
-        for n in range(2):
-            i = pair + n
-            parts = [v[:, n * width : (n + 1) * width] + b for v, b in zip(both, biases)]
-            keep = mask[i : i + 1, :]
-            mixed[0, pl.ds(i, h, stride=OWN), :] = keep * sigmoid(parts[1]) * parts[0]
-            mixed[1, pl.ds(i, h, stride=OWN), :] = keep * sigmoid(parts[3]) * parts[2]
-            gate[:, i * width : (i + 1) * width] = sigmoid(parts[4])
-    send[:, 0:16, :] = mixed[0].reshape(rows // 16, 16, width).astype(BF16)
-    send[:, 16:32, :] = mixed[1].reshape(rows // 16, 16, width).astype(BF16)
-
-
-def finish(u, z, summed, gate, out_weight, columns, mixed):
+    biases = broadcast_columns(columns, u * EACH + 2, 4, width)
+    turned = [proj_weight[:, n * h : (n + 1) * h].T for n in range(4)]
+    halves = [mask[i : i + 1, :] * 0.5 for i in range(OWN)]
+    joined = [norm[:, pair * width : (pair + 2) * width] for pair in range(0, OWN, 2)]
+    for side in range(2):
+        for pair in range(0, OWN, 2):
+            value, gating = [jnp.dot(turned[2 * side + n], joined[pair // 2], preferred_element_type=F32) for n in (0, 1)]
+            for n in range(2):
+                i, at = pair + n, slice(n * width, (n + 1) * width)
+                weight = halves[i] + halves[i] * jnp.tanh(0.5 * (gating[:, at] + biases[2 * side + 1]))
+                mixed[side, pl.ds(i, h, stride=OWN), :] = weight * (value[:, at] + biases[2 * side])
+        send[:, side * 16 : (side + 1) * 16, :] = mixed[side].reshape(rows // 16, 16, width).astype(BF16)
+
+
+def finish(u, z, summed, gate, turned, columns, mixed):
     width = z[0].shape[1]
     gain, offset, bias = broadcast_columns(columns, u * EACH + 7, 3, width)
-    turned = out_weight.T
     mixed[...] = summed[...].astype(F32).reshape(mixed.shape)
     results = []
     for pair in range(0, OWN, 2):
@@ -101,20 +101,17 @@
 
 
 def first_kernel(
-    pair, mask, pw, gw, pb, gb, ob, ns, no, send, gate, turned, columns, keep, pair_in, mask_in, pw_in, gw_in, pb_in, gb_in, ob_in, ns_in, no_in, rows, arrived, mixed
+    pair, mask, pw, gw, pb, gb, ob, ns, no, send, norm, turned, columns, keep, gw_in, pair_in, mask_in, pw_in, pb_in, gb_in, ob_in, ns_in, no_in, rows, arrived, mixed
 ):
-    moves = [(pair, pair_in), (pb, pb_in), (gb, gb_in), (ob, ob_in), (ns, ns_in), (no, no_in)]
-    moves += [(pw.at[0], pw_in), (gw.at[0], gw_in), (mask, mask_in)]
+    moves = [(pair, pair_in), (pw.at[0], pw_in), (ns, ns_in), (no, no_in), (pb, pb_in), (gb, gb_in), (ob, ob_in)]
+    moves += [(mask, mask_in), (gw.at[0], gw_in)]
     moves = [pltpu.make_async_copy(a, b, arrived.at[n]) for n, (a, b) in enumerate(moves)]
     for move in moves:
         move.start()
-    moves[0].wait()
+    for move in moves:
+        move.wait()
     width = pair.shape[1]
     z = [pair_in[i].T for i in range(OWN)]
-    for i in range(OWN):
-        turned[:, i * width : (i + 1) * width] = z[i]
-    for move in moves[1:6]:
-        move.wait()
     h = pw.shape[2] // 4
     for u in range(2):
         found = [ns_in[u, 0:1, :], no_in[u, 0:1, :]] + [pb_in[u : u + 1, n * h : (n + 1) * h] for n in range(4)]
@@ -122,31 +119,55 @@
         for n, row in enumerate(found):
             rows[u * EACH + n : u * EACH + n + 1, :] = row
     columns[...] = rows[...].T
-    for move in moves[6:]:
-        move.wait()
     keep[0:OWN, :] = mask_in[...].astype(F32)
-    project(0, [v.astype(F32) for v in z], keep, pw_in[...], gw_in[...], columns, send, gate, mixed)
-
-
-def middle_kernel(summed, old, old_gate, columns, keep, pw, gw, ow, send, gate, turned, mixed, mixed_back):
+    normalise(0, z, columns, norm, turned, width)
+    project(0, norm, keep, pw_in[...], columns, send, mixed)
+
+
+def normalise(u, z, columns, norm, turned, width):
+    gain, offset = broadcast_columns(columns, u * EACH, 2, width)
+    for i in range(OWN):
+        at = slice(i * width, (i + 1) * width)
+        turned[:, at] = z[i]
+        norm[:, at] = layer_norm(z[i].astype(F32), gain, offset).astype(BF16)
+
+
+def middle_kernel(summed, old, old_gate, columns, keep, pw, ow, send, norm, turned, mixed, mixed_back):
     width = keep.shape[1]
-    z = finish(0, [old[:, i * width : (i + 1) * width] for i in range(OWN)], summed, old_gate, ow[0], columns, mixed_back)
-    for i in range(OWN):
-        turned[:, i * width : (i + 1) * width] = z[i]
-    project(1, [v.astype(F32) for v in z], keep, pw[1], gw[1], columns, send, gate, mixed)
-
-
-def last_kernel(summed, old, old_gate, columns, ow, out, mixed_back):
+    z = [old[:, i * width : (i + 1) * width] for i in range(OWN)]
+    z = finish(0, z, summed, old_gate, ow[0].T, columns, mixed_back)
+    normalise(1, z, columns, norm, turned, width)
+    project(1, norm, keep, pw[1], columns, send, mixed)
+
+
+def last_kernel(summed, old, old_gate, columns, weight, out, mixed_back):
     width = out.shape[1]
-    z = finish(1, [old[:, i * width : (i + 1) * width] for i in range(OWN)], summed, old_gate, ow[1], columns, mixed_back)
+    z = [old[:, i * width : (i + 1) * width] for i in range(OWN)]
+    z = finish(1, z, summed, old_gate, weight[...], columns, mixed_back)
     for i in range(OWN):
         out[i] = z[i].T
 
 
-def triangle_kernel(incoming, sides, out):
-    left, right = [unpack(sides[:, n : n + 16, :].astype(F32)) for n in (0, 16)]
+def triangle(incoming, sides, out):
+    left, right = [[v.astype(BF16) for v in unpack(sides[:, n : n + 16, :].astype(F32))] for n in (0, 16)]
     product = over_rows if incoming else over_columns
-    out[...] = pack([product(a.astype(BF16), b.astype(BF16)) for a, b in zip(left, right)]).astype(BF16)
+    out[...] = pack([product(a, b) for a, b in zip(left, right)]).astype(BF16)
+
+
+def output_gate(u, normed, gate_weight, columns, gate):
+    gating = jnp.dot(gate_weight.T, normed[...], preferred_element_type=F32)
+    gate[...] = sigmoid(gating + columns[:, u * EACH + 6 : u * EACH + 7])
+
+
+def outgoing_kernel(sides, normed, gw, columns, out, gate):
+    triangle(False, sides, out)
+    output_gate(0, normed, gw[...], columns, gate)
+
+
+def incoming_kernel(sides, normed, gw, columns, ow, out, gate, turned):
+    triangle(True, sides, out)
+    output_gate(1, normed, gw[1], columns, gate)
+    turned[...] = ow[1].T
 
 
 def call(kernel, outs, scratch, *args, place=pltpu.VMEM):
@@ -168,20 +189,25 @@
 def packed_updates(count, pair_rep, pair_mask, pw, pb, gw, gb, ow, ob, ns, no):
     rows_of, width, channels = pair_rep.shape
     flat = (channels, rows_of * width)
-    projected = [((count, 32, width), BF16), (flat, F32), (flat, BF16)]
-    summed = [((count, 16, width), BF16)]
+    square = ((channels, channels), BF16)
+    projected = [((count, 32, width), BF16), (flat, BF16), (flat, BF16)]
+    summed = [((count, 16, width), BF16), (flat, F32)]
     params = [pair_rep, pair_mask, pw, gw, pb, gb, ob, ns, no]
     params = [pltpu.with_memory_space_constraint(v, pltpu.HBM) for v in params]
-    held = [pltpu.VMEM(v.shape[1:] if n in (2, 3) else v.shape, v.dtype) for n, v in enumerate(params)]
+    held = [pltpu.VMEM(v.shape[1:] if n == 2 else v.shape, v.dtype) for n, v in enumerate(params) if n != 3]
     held += [pltpu.VMEM((2 * EACH, channels), F32), pltpu.SemaphoreType.DMA((len(params),))]
     back = pltpu.VMEM((OWN * channels, width), F32)
     mixed = pltpu.VMEM((2, OWN * channels, width), F32)
-    kept = [((channels, 2 * EACH), F32), ((2 * OWN, width), F32)]
-    send, gate, turned, columns, keep = call(first_kernel, projected + kept, held + [mixed], *params, place=pltpu.HBM)
-    (send,) = call(functools.partial(triangle_kernel, False), summed, [], exchange(send))
-    send, gate, turned = call(middle_kernel, projected, [mixed, back], exchange(send), turned, gate, columns, keep, pw, gw, ow)
-    (send,) = call(functools.partial(triangle_kernel, True), summed, [], exchange(send))
-    (out,) = call(last_kernel, [(pair_rep.shape, BF16)], [back], exchange(send), turned, gate, columns, ow)
+    kept = [((channels, 2 * EACH), F32), ((2 * OWN, width), F32), square]
+    send, norm, turned, columns, keep, gw0 = call(
+        first_kernel, projected + kept, held + [mixed], *params, place=pltpu.HBM
+    )
+    send, gate = call(outgoing_kernel, summed, [], exchange(send), norm, gw0, columns)
+    send, norm, turned = call(
+        middle_kernel, projected, [mixed, back], exchange(send), turned, gate, columns, keep, pw, ow
+    )
+    send, gate, weight = call(incoming_kernel, summed + [square], [], exchange(send), norm, gw, columns, ow)
+    (out,) = call(last_kernel, [(pair_rep.shape, BF16)], [back], exchange(send), turned, gate, columns, weight)
     return out
 
 

time: 55.2 us -> 55.2 us (level)
  no operation moved by 1% of the time
where the time goes in v2:
time: 55.2 us; the launch traced here: 55 us
  blocking collectives  51 us (92%)
  Pallas kernels  3.94 us (7%)
    all_to_all x4, blocking collectives, exchange(): lax.all_to_all(blocks, PEERS, split_axis=0, concat_axis=0, tiled=True)  51 us
    pallas_call x5, Pallas kernels, call(): pl.pallas_call(kernel, out_shape=[jax.ShapeDtypeStruct(*o) for o in outs]...  3.94 us

profile of v2, /device:TPU:0, one launch (start us, length us, event | category | flops | bytes accessed | tf_op | source)
XLA Modules:
  0.0 55.0 jit_solution(16775194995088679352)
XLA Ops:
  0.0 1.6 %shard_map.100 = (bf16[32,32,128]{2,1,0:T(8,128)(2,1)S(1)}, bf16[128,512]{1,0:T(8,128)(2,1)S(1)}, bf16[128,512]{1,0:T(8,128)(2,1)S(1)}, f32[128,32]{1,0:T(8,128)...) custom-call(bf16[4,128,128]{2,1,0:T(8,128)(2,1)} %pair.1, s32[4,128]{1,0:T(4,128)} %mask.1, ...), custom_call_target="tpu_custom_call" | custom-call | tf_op jit(solution)/shard_map/pallas_call | solution.py:175
  1.6 17.7 %all_to_all.20.sides = bf16[32,32,128]{2,1,0:T(8,128)(2,1)S(1)} all-to-all(bf16[32,32,128]{2,1,0:T(8,128)(2,1)S(1)} %get-tuple-element.19), channel_id=1, replica_groups=mesh['grp'=1,'row'=32,'ka'=1] {'row','ka'}, dimensions={0} | all-to-all | bytes 524288 | tf_op jit(solution)/shard_map/all_to_all | solution.py:186
  19.3 0.0 copy-start
  19.3 0.3 shard_map.101
  19.6 0.0 copy-start.1
  19.6 10.4 %all_to_all.21.summed = bf16[32,16,128]{2,1,0:T(8,128)(2,1)S(1)} all-to-all(bf16[32,16,128]{2,1,0:T(8,128)(2,1)S(1)} %get-tuple-element.23), channel_id=1, replica_groups=mesh['grp'=1,'row'=32,'ka'=1] {'row','ka'}, dimensions={0} | all-to-all | bytes 262144 | tf_op jit(solution)/shard_map/all_to_all | solution.py:186
  30.1 0.0 copy-done
  30.1 0.0 copy-done.1
  30.1 0.7 %shard_map.102 = (bf16[32,32,128]{2,1,0:T(8,128)(2,1)S(1)}, bf16[128,512]{1,0:T(8,128)(2,1)S(1)}, bf16[128,512]{1,0:T(8,128)(2,1)S(1)}) custom-call(bf16[32,16,128]{2,1,0:T(8,128)(2,1)S(1)} %all_to_all.21.summed, bf16[128,512]{1,0:T(8,128)(2,1)S(1)} %get-tuple-element.24.old, f32[128,512]{1,0:T(8,128)S(1)} %get-tuple-element.25.old_gate, ...), custom_call_target="tpu_custom_call" | custom-call | tf_op jit(solution)/shard_map/pallas_call | solution.py:175
  30.8 0.0 copy-start.2
  30.8 12.4 %all_to_all.22.sides = bf16[32,32,128]{2,1,0:T(8,128)(2,1)S(1)} all-to-all(bf16[32,32,128]{2,1,0:T(8,128)(2,1)S(1)} %get-tuple-element.27), channel_id=1, replica_groups=mesh['grp'=1,'row'=32,'ka'=1] {'row','ka'}, dimensions={0} | all-to-all | bytes 524288 | tf_op jit(solution)/shard_map/all_to_all | solution.py:186
  43.3 0.0 copy-done.2
  43.3 0.3 shard_map.103
  43.6 10.4 %all_to_all.23.summed = bf16[32,16,128]{2,1,0:T(8,128)(2,1)S(1)} all-to-all(bf16[32,16,128]{2,1,0:T(8,128)(2,1)S(1)} %get-tuple-element.29), channel_id=1, replica_groups=mesh['grp'=1,'row'=32,'ka'=1] {'row','ka'}, dimensions={0} | all-to-all | bytes 262144 | tf_op jit(solution)/shard_map/all_to_all | solution.py:186
  54.0 1.0 %shard_map.104 = bf16[4,128,128]{2,1,0:T(8,128)(2,1)} custom-call(bf16[32,16,128]{2,1,0:T(8,128)(2,1)S(1)} %all_to_all.23.summed, bf16[128,512]{1,0:T(8,128)(2,1)S(1)} %get-tuple-element.30.old, f32[128,512]{1,0:T(8,128)S(1)} %get-tuple-element.31.old_gate, f32[128,32]{1,0:T(8,128)S(1)} %get-tuple-element.22.columns, ...), custom_call_target="tpu_custom_call" | custom-call | tf_op jit(solution)/shard_map/pallas_call | solution.py:175
Async XLA Ops:
  19.3 10.8 %copy-start = (bf16[2,128,512]{2,1,0:T(8,128)(2,1)S(1)}, bf16[2,128,512]{2,1,0:T(8,128)(2,1)}, u32[]{:S(2)}) copy-start(bf16[2,128,512]{2,1,0:T(8,128)(2,1)} %pw.3) | copy-start | bytes 786436
  19.6 10.5 %copy-start.1 = (bf16[2,128,128]{2,1,0:T(8,128)(2,1)S(1)}, bf16[2,128,128]{2,1,0:T(8,128)(2,1)}, u32[]{:S(2)}) copy-start(bf16[2,128,128]{2,1,0:T(8,128)(2,1)} %ow.3) | copy-start | bytes 196612
  30.8 12.5 %copy-start.2 = (bf16[2,128,128]{2,1,0:T(8,128)(2,1)S(1)}, bf16[2,128,128]{2,1,0:T(8,128)(2,1)}, u32[]{:S(2)}) copy-start(bf16[2,128,128]{2,1,0:T(8,128)(2,1)} %gw.3) | copy-start | bytes 196612

commit v3 on v0

v3 whole, which is shorter than its diff:
```python
import functools

import jax
import jax.numpy as jnp
from jax import lax
from jax.experimental import pallas as pl
from jax.experimental.pallas import tpu as pltpu
from jax.sharding import PartitionSpec as P

PEERS = ("row", "ka")
ROWS = 4
OWN = 8
CHIPS = (15, 14, 13, 12, 11, 10, 9, 8, 7, 6, 5, 4, 3, 2, 1, 0)
EACH = 16
BF16, F32 = jnp.bfloat16, jnp.float32


def over_rows(a, b):
    return lax.dot_general(a, b, (((0,), (0,)), ((), ())), preferred_element_type=F32)


def over_columns(a, b):
    return lax.dot_general(a, b, (((1,), (1,)), ((), ())), preferred_element_type=F32)


def layer_norm(values, norm_gain, norm_bias):
    average = jnp.mean(values, 0, keepdims=True)
    centred = values - average
    variance = jnp.mean(centred * centred, 0, keepdims=True)
    return centred * lax.rsqrt(variance + 1e-05) * norm_gain + norm_bias


def pack(blocks):
    channels, width = blocks[0].shape
    tiles = [b.reshape(channels // OWN, OWN, width) for b in blocks]
    return jnp.stack(tiles, 1).reshape(channels // OWN, ROWS * OWN, width)


def unpack(packed):
    count, _, width = packed.shape
    tiles = packed.reshape(count, ROWS, OWN, width)
    return [tiles[:, i].reshape(count * OWN, width) for i in range(ROWS)]


def sigmoid(x):
    return 0.5 * jnp.tanh(0.5 * x) + 0.5


def broadcast_columns(columns, first, many, width):
    held = columns[...]
    return [jnp.broadcast_to(held[:, n : n + 1], (held.shape[0], width)) for n in range(first, first + many)]


def project(u, z, mask, proj_weight, gate_weight, columns, send, gate):
    width = z[0].shape[1]
    h = proj_weight.shape[1] // 4
    gain, offset, *biases = broadcast_columns(columns, u * EACH, 7, width)
    turned = [proj_weight[:, n * h : (n + 1) * h].T for n in range(4)] + [gate_weight.T]
    lefts, rights = [], []
    for pair in range(0, ROWS, 2):
        normed = [layer_norm(z[i], gain, offset).astype(BF16) for i in (pair, pair + 1)]
        normed = jnp.concatenate(normed, 1)
        both = [jnp.dot(w, normed, preferred_element_type=F32) for w in turned]
        for n in range(2):
            i = pair + n
            parts = [v[:, n * width : (n + 1) * width] + b for v, b in zip(both, biases)]
            keep = mask[i : i + 1, :]
            lefts.append((keep * sigmoid(parts[1]) * parts[0]).astype(BF16))
            rights.append((keep * sigmoid(parts[3]) * parts[2]).astype(BF16))
            gate[:, i * width : (i + 1) * width] = sigmoid(parts[4])
    for n, side in enumerate((lefts, rights)):
        send[:, n * ROWS * OWN : (n + 1) * ROWS * OWN, :] = pack([v.astype(F32) for v in side]).astype(BF16)


def finish(u, z, summed, gate, out_weight, columns):
    width = z[0].shape[1]
    gain, offset, bias = broadcast_columns(columns, u * EACH + 7, 3, width)
    turned = out_weight.T
    results = []
    blocks = unpack(summed[...].astype(F32))
    for pair in range(0, ROWS, 2):
        hidden = [layer_norm(blocks[i], gain, offset).astype(BF16) for i in (pair, pair + 1)]
        both = jnp.dot(turned, jnp.concatenate(hidden, 1), preferred_element_type=F32)
        for n in range(2):
            change = both[:, n * width : (n + 1) * width] + bias
            at = slice((pair + n) * width, (pair + n + 1) * width)
            results.append((z[pair + n].astype(F32) + gate[:, at] * change).astype(BF16))
    return results


def first_kernel(
    pair, mask, pw, gw, pb, gb, ob, ns, no, send, gate, turned, columns, keep, pair_in, mask_in, pw_in, gw_in, pb_in, gb_in, ob_in, ns_in, no_in, rows, arrived
):
    moves = [(pair, pair_in), (pb, pb_in), (gb, gb_in), (ob, ob_in), (ns, ns_in), (no, no_in)]
    moves += [(pw.at[0], pw_in), (gw.at[0], gw_in), (mask, mask_in)]
    moves = [pltpu.make_async_copy(a, b, arrived.at[n]) for n, (a, b) in enumerate(moves)]
    for move in moves:
        move.start()
    moves[0].wait()
    width = pair.shape[1]
    z = [pair_in[i].T for i in range(ROWS)]
    for i in range(ROWS):
        turned[:, i * width : (i + 1) * width] = z[i]
    for move in moves[1:6]:
        move.wait()
    h = pw.shape[2] // 4
    for u in range(2):
        found = [ns_in[u, 0:1, :], no_in[u, 0:1, :]] + [pb_in[u : u + 1, n * h : (n + 1) * h] for n in range(4)]
        found += [gb_in[u : u + 1, :], ns_in[u, 1:2, :], no_in[u, 1:2, :], ob_in[u : u + 1, :]]
        for n, row in enumerate(found):
            rows[u * EACH + n : u * EACH + n + 1, :] = row
    columns[...] = rows[...].T
    for move in moves[6:]:
        move.wait()
    keep[0:ROWS, :] = mask_in[...].astype(F32)
    project(0, [v.astype(F32) for v in z], keep, pw_in[...], gw_in[...], columns, send, gate)


def middle_kernel(summed, old, old_gate, columns, keep, pw, gw, ow, send, gate, turned):
    width = keep.shape[1]
    z = finish(0, [old[:, i * width : (i + 1) * width] for i in range(ROWS)], summed, old_gate, ow[0], columns)
    for i in range(ROWS):
        turned[:, i * width : (i + 1) * width] = z[i]
    project(1, [v.astype(F32) for v in z], keep, pw[1], gw[1], columns, send, gate)


def last_kernel(summed, old, old_gate, columns, ow, out):
    width = out.shape[1]
    z = finish(1, [old[:, i * width : (i + 1) * width] for i in range(ROWS)], summed, old_gate, ow[1], columns)
    for i in range(ROWS):
        out[i] = z[i].T


def rows_at(chip, core):
    return pl.ds(pl.multiple_of((2 * chip + core) * ROWS * OWN, ROWS * OWN), ROWS * OWN)


def outgoing_kernel(sides, other_right, out, left, right, sums):
    core = lax.axis_index("row") & 1
    depth, count = ROWS * OWN, left.shape[0]
    left[...] = sides[:, :depth, :].astype(F32).reshape(left.shape)
    for n, chip in enumerate(CHIPS):
        right[rows_at(chip, core), :] = sides[n, depth:, :].astype(F32)
        right[rows_at(chip, 1 - core), :] = other_right[n].astype(F32)
    for c in range(OWN):
        a = left[pl.ds(c, count // OWN, stride=OWN), :].astype(BF16)
        b = right[pl.ds(c, 2 * count // OWN, stride=OWN), :].astype(BF16)
        sums[pl.ds(c, count // OWN, stride=OWN), :] = over_columns(a, b)
    out[...] = sums[...].astype(BF16).reshape(out.shape)


def incoming_kernel(sides, own, other, left, right, sums):
    core = lax.axis_index("row") & 1
    depth, count = ROWS * OWN, left.shape[0]
    left[...] = sides[:, :depth, :].astype(F32).reshape(left.shape)
    right[...] = sides[:, depth:, :].astype(F32).reshape(right.shape)
    for c in range(OWN):
        a, b = [v[pl.ds(c, count // OWN, stride=OWN), :].astype(BF16) for v in (left, right)]
        sums[pl.ds(c, 2 * count // OWN, stride=OWN), :] = over_rows(a, b)
    for n, chip in enumerate(CHIPS):
        own[n] = sums[rows_at(chip, core), :]
        other[n] = sums[rows_at(chip, 1 - core), :]


def add_kernel(own, from_other, out):
    out[...] = (own[...] + from_other[...]).astype(BF16)


def call(kernel, outs, scratch, *args, place=pltpu.VMEM):
    in_vmem = pl.BlockSpec(memory_space=pltpu.VMEM)
    return pl.pallas_call(
        kernel,
        out_shape=[jax.ShapeDtypeStruct(*o) for o in outs],
        in_specs=[pl.BlockSpec(memory_space=place)] * len(args),
        out_specs=[in_vmem] * len(outs),
        scratch_shapes=scratch,
        compiler_params=pltpu.CompilerParams(vmem_limit_bytes=24 * 2**20),
    )(*args)


def exchange(blocks):
    return lax.all_to_all(blocks, PEERS, split_axis=0, concat_axis=0, tiled=True)


def among_chips(blocks):
    groups = [[2 * chip + core for chip in CHIPS] for core in range(2)]
    return lax.all_to_all(blocks, "row", split_axis=0, concat_axis=0, axis_index_groups=groups, tiled=True)


def to_other_core(values):
    return lax.ppermute(values, "row", [(n, n ^ 1) for n in range(2 * len(CHIPS))])


def packed_updates(count, pair_rep, pair_mask, pw, pb, gw, gb, ow, ob, ns, no):
    rows_of, width, channels = pair_rep.shape
    chips, depth = count // 2, ROWS * OWN
    flat = (channels, rows_of * width)
    projected = [((chips, 2 * depth, width), BF16), (flat, F32), (flat, BF16)]
    summed = (chips, depth, width)
    params = [pair_rep, pair_mask, pw, gw, pb, gb, ob, ns, no]
    params = [pltpu.with_memory_space_constraint(v, pltpu.HBM) for v in params]
    held = [pltpu.VMEM(v.shape[1:] if n in (2, 3) else v.shape, v.dtype) for n, v in enumerate(params)]
    held += [pltpu.VMEM((2 * EACH, channels), F32), pltpu.SemaphoreType.DMA((len(params),))]
    half, whole = [pltpu.VMEM((n * chips * depth, width), F32) for n in (1, 2)]
    kept = [((channels, 2 * EACH), F32), ((2 * ROWS, width), F32)]
    send, gate, turned, columns, keep = call(first_kernel, projected + kept, held, *params, place=pltpu.HBM)
    sides = among_chips(send)
    other = to_other_core(sides[:, depth:])
    (send,) = call(outgoing_kernel, [(summed, BF16)], [half, whole, half], sides, other)
    send, gate, turned = call(middle_kernel, projected, [], among_chips(send), turned, gate, columns, keep, pw, gw, ow)
    own, other = call(incoming_kernel, [(summed, F32)] * 2, [half, half, whole], among_chips(send))
    (send,) = call(add_kernel, [(summed, BF16)], [], own, to_other_core(other))
    (out,) = call(last_kernel, [(pair_rep.shape, BF16)], [], among_chips(send), turned, gate, columns, ow)
    return out


def update(pair_t, pair_mask, u, incoming, peers, rows_of, pw, pb, gw, gb, ow, ob, ns, no):
    channels, positions = pair_t.shape
    width = positions // rows_of
    h = pw.shape[2] // 4
    count = peers[0] * peers[1]
    own = h // count
    normed = layer_norm(pair_t, ns[u, 0][:, None], no[u, 0][:, None]).astype(BF16)
    projected = over_rows(jnp.concatenate([pw[u], gw[u]], 1), normed) + jnp.concatenate([pb[u], gb[u]], 0)[:, None]
    parts = [projected[n * h : (n + 1) * h] for n in range(4)]
    gating = jax.nn.sigmoid(projected[4 * h :])
    mask = pair_mask.astype(F32).reshape(1, positions)
    left = (mask * jax.nn.sigmoid(parts[1]) * parts[0]).astype(BF16)
    right = (mask * jax.nn.sigmoid(parts[3]) * parts[2]).astype(BF16)
    sides = exchange(jnp.stack([v.reshape(count, own, rows_of, width) for v in (left, right)], 1))
    sides = sides.reshape(peers[0], peers[1], 2, own, rows_of, width)
    sides = sides.transpose(2, 3, 0, 4, 1, 5).reshape(2, own, peers[0] * rows_of, peers[1] * width)
    form = "cki,ckj->cij" if incoming else "cik,cjk->cij"
    summed = jnp.einsum(form, sides[0], sides[1], preferred_element_type=F32).astype(BF16)
    summed = summed.reshape(own, peers[0], rows_of, peers[1], width).transpose(1, 3, 0, 2, 4)
    summed = exchange(summed.reshape(count, own, rows_of, width)).reshape(h, positions).astype(F32)
    hidden = layer_norm(summed, ns[u, 1][:, None], no[u, 1][:, None]).astype(BF16)
    change = over_rows(ow[u], hidden) + ob[u][:, None]
    return (pair_t + gating * change).astype(BF16)


def plain_updates(peers, pair_rep, pair_mask, *params):
    rows_of, width, channels = pair_rep.shape
    pair_t = pair_rep.reshape(rows_of * width, channels).T
    for u in range(2):
        pair_t = update(pair_t.astype(F32), pair_mask, u, u == 1, peers, rows_of, *params)
    return pair_t.T.reshape(rows_of, width, channels)


def solution(mesh):
    peers = (mesh.shape["row"], mesh.shape["ka"])
    count = peers[0] * peers[1]

    def on_device(pair_rep, pair_mask, *params):
        rows_of, width, channels = pair_rep.shape
        hidden = params[0].shape[2] // 4
        fits = peers[1] == 1 and rows_of == ROWS and 2 * hidden == OWN * count and count == 2 * len(CHIPS)
        if fits and channels == hidden == 128 and width == 2 * len(CHIPS) * ROWS:
            return packed_updates(count, pair_rep, pair_mask, *params)
        return plain_updates(peers, pair_rep, pair_mask, *params)

    split = P(("grp", "row"), "ka", None)
    in_specs = (split, P(("grp", "row"), "ka")) + (P(),) * 8
    return jax.shard_map(on_device, mesh=mesh, in_specs=in_specs, out_specs=split, check_vma=False)
```

time: 55.2 us -> 58 us (1.051)
  waiting for transfers between devices: 0 us -> 2.86 us
  blocking collectives: 51 us -> 50.4 us
    ppermute x0 -> x2, waiting for transfers between devices: none -> 2.86 us  [to_other_core(): lax.ppermute(values, 'row', [(n, n ^ 1) for n in range(2 * len(CHIPS))])]
    pallas_call x5 -> x6, Pallas kernels: 3.96 us -> 4.14 us  [call(): pl.pallas_call(kernel, out_shape=[jax.ShapeDtypeStruct(*o) for o in outs]...]
  transfers between devices with their start and end apart: 0 -> 2, of which waited for: 0 -> 2; matrix products, arithmetic and copies ran while one was open for 0% -> 0% of each run, Pallas kernels for 0% -> 0%
where the time goes in v3:
time: 58 us; the launch traced here: 57.7 us
  blocking collectives  50.4 us (87%)
  Pallas kernels  4.14 us (7%)
  waiting for transfers between devices  2.86 us (5%)
    all_to_all x4, blocking collectives, among_chips(): lax.all_to_all(blocks, 'row', split_axis=0, concat_axis=0, axis_index_gro...  50.4 us
    pallas_call x6, Pallas kernels, call(): pl.pallas_call(kernel, out_shape=[jax.ShapeDtypeStruct(*o) for o in outs]...  4.14 us
    ppermute x2, waiting for transfers between devices, to_other_core(): lax.ppermute(values, 'row', [(n, n ^ 1) for n in range(2 * len(CHIPS))])  2.86 us
  transfers between devices with their start and end apart: 2, of which 2 were waited for; matrix products, arithmetic and copies ran while one was open for 0% of the time, Pallas kernels for 0%

profile of v3, /device:TPU:0, one launch (start us, length us, event | category | flops | bytes accessed | tf_op | source)
XLA Modules:
  0.0 57.7 jit_solution(12693285131378169179)
XLA Ops:
  0.0 1.7 %shard_map.100 = (bf16[16,64,128]{2,1,0:T(8,128)(2,1)S(1)}, f32[128,512]{1,0:T(8,128)S(1)}, bf16[128,512]{1,0:T(8,128)(2,1)S(1)}, f32[128,32]{1,0:T(8,128)S(1)}, f32[8,128]{1,0:T(8,128)S(1)}) custom-call(bf16[4,128,128]{2,1,0:T(8,128)(2,1)} %pair.1, s32[4,128]{1,0:T(4,128)} %mask.1, bf16[2,128,512]{2,1,0:T(8,128)(2,1)} %pw.3, bf16[2,128,128]{2,1,0:T(8,128)(2,1)} %gw.3, ...), custom_call_target="tpu_custom_call" | custom-call | tf_op jit(solution)/shard_map/pallas_call | solution.py:171
  1.7 16.1 %all_to_all.20.sides = bf16[16,64,128]{2,1,0:T(8,128)(2,1)S(1)} all-to-all(bf16[16,64,128]{2,1,0:T(8,128)(2,1)S(1)} %get-tuple-element.15), channel_id=1, replica_groups={{30,28,26,24,22,20,18,16,14,12,10,8,6,4,2,0},{31,29,27,25,23,21,19,17,1..., dimensions={0} | all-to-all | bytes 524288 | tf_op jit(solution)/shard_map/all_to_all | solution.py:187
  17.8 0.1 collective-permute-start
  17.9 1.3 %collective-permute-done.other_right = bf16[16,32,128]{2,1,0:T(8,128)(2,1)S(1)} collective-permute-done((bf16[16,32,128]{2,1,0:T(8,128)(2,1)S(1)}, bf16[16,32,128]{2,1,0:T(8,128)(2,1)S(1)}, u32[]{:S(2)}, u32[]{:S(2)}) %collective-permute-start) | collective-permute-done | bytes 131104 | tf_op jit(solution)/shard_map/ppermute | solution.py:191
  19.2 0.0 copy-start.1
  19.2 0.0 copy-start.2
  19.2 0.3 shard_map.101
  19.6 0.0 copy-start
  19.6 10.8 %all_to_all.21.summed = bf16[16,32,128]{2,1,0:T(8,128)(2,1)S(1)} all-to-all(bf16[16,32,128]{2,1,0:T(8,128)(2,1)S(1)} %shard_map.101), channel_id=1, replica_groups={{30,28,26,24,22,20,18,16,14,12,10,8,6,4,2,0},{31,29,27,25,23,21,19,17,1..., dimensions={0} | all-to-all | bytes 262144 | tf_op jit(solution)/shard_map/all_to_all | solution.py:187
  30.4 0.0 copy-done.1
  30.4 0.0 copy-done.2
  30.4 0.0 copy-done
  30.4 0.8 %shard_map.102 = (bf16[16,64,128]{2,1,0:T(8,128)(2,1)S(1)}, f32[128,512]{1,0:T(8,128)S(1)}, bf16[128,512]{1,0:T(8,128)(2,1)S(1)}) custom-call(bf16[16,32,128]{2,1,0:T(8,128)(2,1)S(1)} %all_to_all.21.summed, bf16[128,512]{1,0:T(8,128)(2,1)S(1)} %get-tuple-element.16.old, f32[128,512]{1,0:T(8,128)S(1)} %get-tuple-element.17.old_gate, ...), custom_call_target="tpu_custom_call" | custom-call | tf_op jit(solution)/shard_map/pallas_call | solution.py:171
  31.2 12.9 %all_to_all.22.sides = bf16[16,64,128]{2,1,0:T(8,128)(2,1)S(1)} all-to-all(bf16[16,64,128]{2,1,0:T(8,128)(2,1)S(1)} %get-tuple-element.20), channel_id=1, replica_groups={{30,28,26,24,22,20,18,16,14,12,10,8,6,4,2,0},{31,29,27,25,23,21,19,17,1..., dimensions={0} | all-to-all | bytes 524288 | tf_op jit(solution)/shard_map/all_to_all | solution.py:187
  44.1 0.3 shard_map.103
  44.4 0.1 collective-permute-start.1
  44.5 1.5 %collective-permute-done.1.from_other = f32[16,32,128]{2,1,0:T(8,128)S(1)} collective-permute-done((f32[16,32,128]{2,1,0:T(8,128)S(1)}, f32[16,32,128]{2,1,0:T(8,128)S(1)}, u32[]{:S(2)}, u32[]{:S(2)}) %collective-permute-start.1) | collective-permute-done | bytes 262176 | tf_op jit(solution)/shard_map/ppermute | solution.py:191
  46.1 10.6 %all_to_all.23.summed = bf16[16,32,128]{2,1,0:T(8,128)(2,1)S(1)} all-to-all(bf16[16,32,128]{2,1,0:T(8,128)(2,1)S(1)} %shard_map.104), channel_id=1, replica_groups={{30,28,26,24,22,20,18,16,14,12,10,8,6,4,2,0},{31,29,27,25,23,21,19,17,1..., dimensions={0} | all-to-all | bytes 262144 | tf_op jit(solution)/shard_map/all_to_all | solution.py:187
  56.7 1.0 %shard_map.105 = bf16[4,128,128]{2,1,0:T(8,128)(2,1)} custom-call(bf16[16,32,128]{2,1,0:T(8,128)(2,1)S(1)} %all_to_all.23.summed, bf16[128,512]{1,0:T(8,128)(2,1)S(1)} %get-tuple-element.23.old, f32[128,512]{1,0:T(8,128)S(1)} %get-tuple-element.24.old_gate, f32[128,32]{1,0:T(8,128)S(1)} %get-tuple-element.18.columns, bf16[2,128,128]{2,1,0:T(8,128)(2,1)S(1)} %copy-done.2), custom_call_target="tpu_custom_call" | custom-call | tf_op jit(solution)/shard_map/pallas_call | solution.py:171
  (2 shorter events, 0.0 us)
Async XLA Ops:
  17.8 1.4 %collective-permute-start = (bf16[16,32,128]{2,1,0:T(8,128)(2,1)S(1)}, bf16[16,32,128]{2,1,0:T(8,128)(2,1)S(1)}, u32[]{:S(2)}, u32[]{:S(2)}) collective-permute-start(bf16[16,32,128]{2,1,0:T(8,128)(2,1)S(1)} %slice.4), channel_id=1, source_target_pairs={{0,1},{1,0},{2,3},{3,2},{4,5},{5,4},{6,7},{7,6},{8,9},{9,8},{10,11... | collective-permute-start | bytes 393224 | tf_op jit(solution)/shard_map/ppermute | solution.py:191
  19.2 11.1 %copy-start.1 = (bf16[2,128,128]{2,1,0:T(8,128)(2,1)S(1)}, bf16[2,128,128]{2,1,0:T(8,128)(2,1)}, u32[]{:S(2)}) copy-start(bf16[2,128,128]{2,1,0:T(8,128)(2,1)} %gw.3) | copy-start | bytes 196612
  19.2 11.1 %copy-start.2 = (bf16[2,128,128]{2,1,0:T(8,128)(2,1)S(1)}, bf16[2,128,128]{2,1,0:T(8,128)(2,1)}, u32[]{:S(2)}) copy-start(bf16[2,128,128]{2,1,0:T(8,128)(2,1)} %ow.3) | copy-start | bytes 196612
  19.6 10.8 %copy-start = (bf16[2,128,512]{2,1,0:T(8,128)(2,1)S(1)}, bf16[2,128,512]{2,1,0:T(8,128)(2,1)}, u32[]{:S(2)}) copy-start(bf16[2,128,512]{2,1,0:T(8,128)(2,1)} %pw.3) | copy-start | bytes 786436
  44.4 1.6 %collective-permute-start.1 = (f32[16,32,128]{2,1,0:T(8,128)S(1)}, f32[16,32,128]{2,1,0:T(8,128)S(1)}, u32[]{:S(2)}, u32[]{:S(2)}) collective-permute-start(f32[16,32,128]{2,1,0:T(8,128)S(1)} %get-tuple-element.22), channel_id=1, source_target_pairs={{0,1},{1,0},{2,3},{3,2},{4,5},{5,4},{6,7},{7,6},{8,9},{9,8},{10,11... | collective-permute-start | bytes 786440 | tf_op jit(solution)/shard_map/ppermute | solution.py:191
